TPU v7x, 32 devices: a whole 2x2x4 slice. The times are simulated.
32 devices in a mesh: blocks: 8 (over y, x, core), phi: 4 (over z).
Axes of the slice: x: 2, y: 2, z: 4, core: 2. Of those that a mesh axis runs over, the one named last changes fastest.
Arguments:
- field: float32 [3, 128, 64, 512], P(None, 'blocks', 'phi'), may hold values from -6 to 6
- velocity: float32 [3, 128, 64, 512], P(None, 'blocks', 'phi'), may hold values from -6 to 6
- strip_shift: int32 [128], P('blocks'), may hold values from 0 to 6, as said below
- strip_frac: float32 [128], P('blocks'), may hold values from 0 to 1
- edge_shift: int32 [2], replicated, may hold values from 0 to 6, as said below
- edge_frac: float32 [2], replicated, may hold values from 0 to 1
Outputs:
- advected: float32 [3, 128, 64, 512], P(None, 'blocks', 'phi')
Inputs may be any that keep to these rules, and one draw needn't show every extreme that they name: `strip_shift`: some strip has a shift of exactly 6 and some strip a shift of 0. `edge_shift`: exactly one of the two boundary offsets equals 6; the other is smaller.
All inputs are finite; a program needn't handle non-finite values.
Results may differ from a plain program's by a relative error of at most 0.00002.
Values sent between devices are 32-bit elements; how exact they have to be, the bound alone decides.
A program may use at most 128 MiB of HBM per device.

v0:
```python
import jax
import jax.numpy as jnp
from jax import lax
from jax.sharding import PartitionSpec as P

KMAX = 6


COURANT = 0.4


def with_halo(shard, sides, width):
    for axis, dim in sides:
        peers, length = (lax.axis_size(axis), shard.shape[dim])
        up = [(i, (i + 1) % peers) for i in range(peers)]
        down = [(j, i) for i, j in up]
        last = lax.slice_in_dim(shard, length - width, length, axis=dim)
        first = lax.slice_in_dim(shard, 0, width, axis=dim)
        before = lax.ppermute(last, axis, up)
        after = lax.ppermute(first, axis, down)
        shard = jnp.concatenate([before, shard, after], axis=dim)
    return shard


def from_behind(shard, axis, by):
    peers = lax.axis_size(axis)
    return lax.ppermute(shard, axis, [(i, (i + by) % peers) for i in range(peers)])


def below(values):
    return jnp.roll(values, 1, axis=-1)


def above(values):
    return jnp.roll(values, -1, axis=-1)


def ct_update(padded):
    field_x, field_y, field_z = (padded[0], padded[1], padded[2])
    flow_x, flow_y, flow_z = (padded[3], padded[4], padded[5])
    zedge_fx = 0.5 * (field_x[1:, 1:] + field_x[1:, :-1])
    zedge_fy = 0.5 * (field_y[1:, 1:] + field_y[:-1, 1:])
    zedge_vx = 0.25 * (flow_x[1:, 1:] + flow_x[:-1, 1:] + flow_x[1:, :-1] + flow_x[:-1, :-1])
    zedge_vy = 0.25 * (flow_y[1:, 1:] + flow_y[:-1, 1:] + flow_y[1:, :-1] + flow_y[:-1, :-1])
    emf_z = zedge_vy * zedge_fx - zedge_vx * zedge_fy
    middle_fx = field_x[:, 1:-1]
    middle_fz = field_z[:, 1:-1]
    middle_vx = flow_x[:, 1:-1]
    middle_vz = flow_z[:, 1:-1]
    yedge_fx = 0.5 * (middle_fx[1:] + below(middle_fx[1:]))
    yedge_fz = 0.5 * (middle_fz[1:] + middle_fz[:-1])
    paired_vx = middle_vx[1:] + middle_vx[:-1]
    paired_vz = middle_vz[1:] + middle_vz[:-1]
    yedge_vx = 0.25 * (paired_vx + below(paired_vx))
    yedge_vz = 0.25 * (paired_vz + below(paired_vz))
    emf_y = yedge_vx * yedge_fz - yedge_vz * yedge_fx
    radial_fy = field_y[1:-1]
    radial_fz = field_z[1:-1]
    radial_vy = flow_y[1:-1]
    radial_vz = flow_z[1:-1]
    xedge_fy = 0.5 * (radial_fy[:, 1:] + below(radial_fy[:, 1:]))
    xedge_fz = 0.5 * (radial_fz[:, 1:] + radial_fz[:, :-1])
    couple_vy = radial_vy[:, 1:] + radial_vy[:, :-1]
    couple_vz = radial_vz[:, 1:] + radial_vz[:, :-1]
    xedge_vy = 0.25 * (couple_vy + below(couple_vy))
    xedge_vz = 0.25 * (couple_vz + below(couple_vz))
    emf_x = xedge_vz * xedge_fy - xedge_vy * xedge_fz
    radial_count = emf_x.shape[0]
    azimuth_count = emf_y.shape[1]
    new_x = field_x[1:-1, 1:-1] - COURANT * (
        emf_z[:radial_count, 1:]
        - emf_z[:radial_count, :azimuth_count]
        - (above(emf_y[:radial_count]) - emf_y[:radial_count])
    )
    new_y = field_y[1:-1, 1:-1] - COURANT * (
        above(emf_x[:, :azimuth_count])
        - emf_x[:, :azimuth_count]
        - (emf_z[1:, :azimuth_count] - emf_z[:radial_count, :azimuth_count])
    )
    new_z = field_z[1:-1, 1:-1] - COURANT * (
        emf_y[1:] - emf_y[:radial_count] - (emf_x[:, 1:] - emf_x[:, :azimuth_count])
    )
    return jnp.stack([new_x, new_y, new_z])


def blend_rows(extended, near_start, far_start, weight, length):
    leading = lax.dynamic_slice_in_dim(extended, near_start, length, axis=1)
    trailing = lax.dynamic_slice_in_dim(extended, far_start, length, axis=1)
    return (1.0 - weight) * leading + weight * trailing


def body(field, velocity, strip_shift, strip_frac, edge_shift, edge_frac):
    azimuth = field.shape[2]
    stacked = jnp.concatenate([field, velocity], axis=0)
    first_block = lax.axis_index("blocks") == 0
    last_block = lax.axis_index("blocks") == lax.axis_size("blocks") - 1
    inner_shift = edge_shift[0]
    outer_shift = edge_shift[1]
    padded = with_halo(stacked, (("blocks", 1), ("phi", 2)), 1)
    low_rows = padded[:, 0]
    high_rows = padded[:, -1]
    taken_low = from_behind(low_rows[:, azimuth - KMAX - 1 : azimuth + 1], "phi", 1)
    taken_high = from_behind(high_rows[:, 1 : KMAX + 3], "phi", -1)
    extended_low = jnp.concatenate([taken_low, low_rows[:, 1:]], axis=1)
    extended_high = jnp.concatenate([high_rows[:, : azimuth + 1], taken_high], axis=1)
    span = azimuth + 2
    remapped_low = blend_rows(
        extended_low, KMAX + 1 - inner_shift, KMAX - inner_shift, edge_frac[0], span
    )
    remapped_high = blend_rows(extended_high, outer_shift, outer_shift + 1, edge_frac[1], span)
    padded = padded.at[:, 0].set(jnp.where(first_block, remapped_low, low_rows))
    padded = padded.at[:, -1].set(jnp.where(last_block, remapped_high, high_rows))
    updated = ct_update(padded)
    received = from_behind(updated[:, :, azimuth - KMAX - 1 :], "phi", 1)
    extended = jnp.concatenate([received, updated], axis=2)

    def one_strip(rows, shift, weight):
        return blend_rows(rows, KMAX + 1 - shift, KMAX - shift, weight, azimuth)

    return jax.vmap(one_strip, in_axes=(1, 0, 0), out_axes=1)(extended, strip_shift, strip_frac)


def solution(mesh):
    placed = (
        P(None, "blocks", "phi", None),
        P(None, "blocks", "phi", None),
        P("blocks"),
        P("blocks"),
        P(),
        P(),
    )
    return jax.shard_map(
        body, mesh=mesh, in_specs=placed, out_specs=P(None, "blocks", "phi", None), check_vma=False
    )
```

profile of v0, /device:TPU:0, one launch (start us, length us, event | category | flops | bytes accessed | tf_op | source)
XLA Modules:
  0.0 109.2 jit_solution(2533444183082880349)
XLA Ops:
  0.0 2.3 %pad_maximum_fusion.1 = f32[6,16,16,512]{3,2,1,0:T(8,128)S(1)} fusion(f32[3,16,16,512]{3,2,1,0:T(8,128)} %param.11, f32[3,16,16,512]{3,2,1,0:T(8,128)} %param.10), kind=kLoop, calls=%fused_computation.3 | loop fusion | flops 786432 | bytes 6291456 | tf_op jit(solution)/shard_map/concatenate | solution.py:94
  2.4 0.5 collective-permute-start
  2.9 3.0 %collective-permute-start.1 = (f32[6,1,16,512]{3,2,0,1:T(8,128)S(1)}, f32[6,1,16,512]{3,2,0,1:T(8,128)S(1)}, u32[]{:S(2)}, u32[]{:S(2)}) collective-permute-start(f32[6,1,16,512]{3,2,0,1:T(8,128)S(1)} %copy.24), channel_id=1, source_target_pairs={{4,0},{8,4},{12,8},{16,12},{20,16},{24,20},{28,24},{0,28},{5,1},{9... | collective-permute-start | bytes 589832 | tf_op jit(solution)/shard_map/ppermute | solution.py:20
  5.9 3.3 %collective-permute-done = f32[6,1,16,512]{3,2,0,1:T(8,128)S(1)} collective-permute-done((f32[6,1,16,512]{3,2,0,1:T(8,128)S(1)}, f32[6,1,16,512]{3,2,0,1:T(8,128)S(1)}, u32[]{:S(2)}, u32[]{:S(2)}) %collective-permute-start) | collective-permute-done | bytes 196640 | tf_op jit(solution)/shard_map/ppermute | solution.py:19
  9.2 0.0 copy-done.2
  9.2 0.0 copy-done.1
  9.2 0.0 copy-start.3
  9.2 0.4 constant_dynamic-update-slice_fusion.1
  9.6 0.5 collective-permute-done.1
  10.1 1.2 %fusion.50 = (f32[6,18,1,512]{3,2,0,1:T(1,128)}, f32[6,18,1,512]{3,2,0,1:T(1,128)}) fusion(f32[6,18,16,512]{3,2,0,1:T(8,128)S(1)} %constant_dynamic-update-slice_fusion), kind=kLoop, calls=%fused_computation.113 | loop fusion | bytes 884736 | tf_op jit(solution)/shard_map/slice | solution.py:17
  11.3 1.9 %collective-permute-start.2 = (f32[6,18,1,512]{3,2,0,1:T(1,128)}, f32[6,18,1,512]{3,2,0,1:T(1,128)}, u32[]{:S(2)}, u32[]{:S(2)}) collective-permute-start(f32[6,18,1,512]{3,2,0,1:T(1,128)} %get-tuple-element.41), channel_id=1, source_target_pairs={{0,1},{1,2},{2,3},{3,0},{4,5},{5,6},{6,7},{7,4},{8,9},{9,10},{10,1... | collective-permute-start | bytes 663560 | tf_op jit(solution)/shard_map/ppermute | solution.py:19
  13.3 2.0 %collective-permute-start.3 = (f32[6,18,1,512]{3,2,0,1:T(1,128)}, f32[6,18,1,512]{3,2,0,1:T(1,128)}, u32[]{:S(2)}, u32[]{:S(2)}) collective-permute-start(f32[6,18,1,512]{3,2,0,1:T(1,128)} %get-tuple-element.42), channel_id=1, source_target_pairs={{1,0},{2,1},{3,2},{0,3},{5,4},{6,5},{7,6},{4,7},{9,8},{10,9},{11,1... | collective-permute-start | bytes 663560 | tf_op jit(solution)/shard_map/ppermute | solution.py:20
  15.3 0.6 fusion.53
  18.5 0.0 copy-start.4
  18.5 3.0 %collective-permute-done.2 = f32[6,18,1,512]{3,2,0,1:T(1,128)} collective-permute-done((f32[6,18,1,512]{3,2,0,1:T(1,128)}, f32[6,18,1,512]{3,2,0,1:T(1,128)}, u32[]{:S(2)}, u32[]{:S(2)}) %collective-permute-start.2) | collective-permute-done | bytes 221216 | tf_op jit(solution)/shard_map/ppermute | solution.py:19
  21.4 5.1 %collective-permute-done.3 = f32[6,18,1,512]{3,2,0,1:T(1,128)} collective-permute-done((f32[6,18,1,512]{3,2,0,1:T(1,128)}, f32[6,18,1,512]{3,2,0,1:T(1,128)}, u32[]{:S(2)}, u32[]{:S(2)}) %collective-permute-start.3) | collective-permute-done | bytes 221216 | tf_op jit(solution)/shard_map/ppermute | solution.py:20
  26.5 2.1 %pad_maximum_fusion = f32[6,18,18,512]{3,2,0,1:T(8,128)S(1)} fusion(f32[6,18,1,512]{3,2,0,1:T(1,128)} %collective-permute-done.3, f32[6,18,16,512]{3,2,0,1:T(8,128)S(1)} %constant_dynamic-update-slice_fusion, f32[6,18,1,512]{3,2,0,1:T(1,128)} %collective-permute-done.2), kind=kLoop, calls=%fused_computation.2 | loop fusion | flops 1990656 | bytes 7962624 | tf_op jit(solution)/shard_map/concatenate | solution.py:21
  28.6 2.3 %copy-done = f32[6,18,18,512]{3,2,0,1:T(8,128)} copy-done((f32[6,18,18,512]{3,2,0,1:T(8,128)}, f32[6,18,18,512]{3,2,0,1:T(8,128)S(1)}, u32[]{:S(2)}) %copy-start) | copy-done | bytes 3981336
  31.0 0.7 collective-permute-start.4
  31.7 0.0 copy-done.4
  31.7 0.6 fusion.52
  32.9 5.7 %copy.27 = f32[6,18,18,512]{3,2,0,1:T(8,128)} copy(f32[6,18,18,512]{3,2,0,1:T(8,128)} %copy-done) | data formatting | bytes 7962624
  38.6 0.0 collective-permute-done.4
  38.6 2.5 %slice_bitcast_fusion.10 = (f32[6,18,512]{2,1,0:T(8,128)S(1)}, f32[6,18,18,512]{3,2,0,1:T(8,128)}) fusion(f32[6,18,18,512]{3,2,0,1:T(8,128)} %copy.27, f32[6,18,512]{2,1,0:T(8,128)S(1)} %slice_bitcast_fusion.11, s32[]{:T(128)S(6)} %select_n.34, f32[]{:T(128)} %bitcast, s32[]{:T(128)S(6)} %select_n.33, f32[6,17,512]{2,1,0:T(8,128)S(1)} %slice.424, ...), kind=kLoop, calls=%fused_computation.98 | loop fusion | flops 331776 | bytes 1339917 | tf_op jit(solution)/shard_map/squeeze | solution.py:101
  41.1 3.4 %collective-permute-start.5 = (f32[6,8,512]{2,1,0:T(8,128)S(1)}, f32[6,8,512]{2,1,0:T(8,128)S(1)}, u32[]{:S(2)}, u32[]{:S(2)}) collective-permute-start(f32[6,8,512]{2,1,0:T(8,128)S(1)} %slice.427), channel_id=1, source_target_pairs={{0,3},{1,0},{2,1},{3,2},{4,7},{5,4},{6,5},{7,6},{8,11},{9,8},{10,9... | collective-permute-start | bytes 294920 | tf_op jit(solution)/shard_map/ppermute | solution.py:27
  48.0 7.2 %copy.15 = f32[6,18,18,512]{3,1,2,0:T(8,128)} copy(f32[6,18,18,512]{3,2,0,1:T(8,128)} %get-tuple-element.40) | data formatting | bytes 7962624 | tf_op jit(solution)/shard_map/scatter | solution.py:111
  55.2 0.0 collective-permute-done.5
  55.2 1.8 %fusion.35 = f32[6,18,512]{2,1,0:T(8,128)S(1)} fusion(s32[]{:T(128)S(6)} %select_n.38, f32[6,17,512]{2,1,0:T(8,128)S(1)} %bitcast.70, s32[]{:T(128)S(6)} %select_n.37, f32[6,8,512]{2,1,0:T(8,128)S(1)} %collective-permute-done.5, f32[]{:T(128)} %bitcast.7, f32[]{:T(128)S(6)} %sub.78, pred[]{:T(512)S(6)} %eq.7, f32[6,18,18,512]{3,2,0,1:T(8,128)} %copy-done), kind=kLoop, calls=%fused_computation.87 | loop fusion | flops 331776 | bytes 749585 | tf_op jit(solution)/shard_map/jit(_where)/select_n | solution.py:112
  57.1 0.2 reshape.87
  57.2 8.6 %scatter.9 = f32[6,18,18,512]{3,1,2,0:T(8,128)} dynamic-update-slice(f32[6,18,18,512]{3,1,2,0:T(8,128)} %copy.15, f32[6,1,18,512]{3,1,2,0:T(1,128)S(1)} %reshape.87, s32[]{:T(128)} %constant.88.clone.1, s32[]{:T(128)} %constant.97.clone.1, s32[]{:T(128)} %constant.88.clone.1, s32[]{:T(128)} %constant.88.clone.1) | dynamic-update-slice | bytes 442372 | tf_op jit(solution)/shard_map/scatter | solution.py:112
  65.8 2.6 %slice_bitcast_fusion.7 = (f32[16,18,512]{2,0,1:T(8,128)S(1)}, f32[16,18,512]{2,0,1:T(8,128)S(1)}, f32[16,18,512]{2,0,1:T(8,128)S(1)}, f32[16,18,512]{2,0,1:T(8,128)S(1)}) fusion(f32[6,18,18,512]{3,1,2,0:T(8,128)} %scatter.9), kind=kLoop, calls=%fused_computation.43 | loop fusion | bytes 4718592 | tf_op jit(solution)/shard_map/slice | solution.py:59
  68.5 0.1 slice.473
  68.6 0.0 slice-start.1
  68.6 0.1 slice_add_fusion.13
  68.7 0.1 slice.469
  68.8 0.1 slice.478
  68.9 0.6 fusion.16
  69.5 0.2 slice.483
  69.7 0.2 slice-done.1
  69.9 1.1 slice_bitcast_fusion.4
  71.0 0.1 slice.461
  71.1 0.1 slice.460
  71.3 0.3 slice_add_fusion.9
  71.5 0.1 slice.449
  71.7 0.1 slice.457
  71.8 1.0 fusion.9
  72.8 0.2 slice.462
  73.0 0.9 fusion.2
  73.9 1.0 fusion.31
  74.9 0.5 copy.16
  75.5 0.0 copy-start.5
  75.5 0.0 copy-start.6
  75.5 0.5 copy.17
  76.0 0.4 stack.14
  76.4 0.6 pad_maximum_fusion.2
  77.0 0.2 copy.18
  77.3 0.3 collective-permute-start.6
  77.6 18.6 %collective-permute-done.6 = f32[3,16,7,512]{3,1,2,0:T(8,128)S(1)} collective-permute-done((f32[3,16,7,512]{3,1,2,0:T(8,128)S(1)}, f32[3,16,7,512]{3,1,2,0:T(8,128)S(1)}, u32[]{:S(2)}, u32[]{:S(2)}) %collective-permute-start.6) | collective-permute-done | bytes 688160 | tf_op jit(solution)/shard_map/ppermute | solution.py:27
  96.2 0.5 copy.19
  96.7 1.8 %maximum_bitcast_fusion = f32[16,3,23,512]{3,1,0,2:T(4,128)S(1)} fusion(f32[1,16,16,512]{3,0,1,2:T(1,128)S(1)} %stack.14, f32[1,16,16,512]{3,0,1,2:T(1,128)S(1)} %copy.17, f32[1,16,16,512]{3,0,1,2:T(1,128)S(1)} %copy.16, f32[3,16,7,512]{3,0,1,2:T(4,128)S(1)} %copy.19), kind=kLoop, calls=%fused_computation.4 | loop fusion | flops 1695744 | bytes 4521984 | tf_op jit(solution)/shard_map/vmap()/transpose | solution.py:87
  98.6 3.0 %gather_fusion = f32[16,3,16,512]{3,1,2,0:T(4,128)} fusion(f32[16,3,23,512]{3,1,0,2:T(4,128)S(1)} %maximum_bitcast_fusion, s32[16]{0:T(128)S(1)} %get-tuple-element.48), kind=kCustom, calls=%fused_computation | custom fusion | bytes 3145984 | tf_op jit(solution)/shard_map/vmap()/gather | solution.py:87
  101.6 3.0 %gather_fusion.1 = f32[16,3,16,512]{3,1,2,0:T(4,128)} fusion(f32[16,3,23,512]{3,1,0,2:T(4,128)S(1)} %maximum_bitcast_fusion, s32[16]{0:T(128)S(1)} %get-tuple-element.49), kind=kCustom, calls=%fused_computation.1 | custom fusion | bytes 3145984 | tf_op jit(solution)/shard_map/vmap()/gather | solution.py:88
  104.6 3.0 %add_bitcast_fusion = f32[3,16,16,512]{3,0,2,1:T(4,128)S(1)} fusion(f32[16,3,16,512]{3,1,2,0:T(4,128)} %gather_fusion.1, f32[16,3,16,512]{3,1,2,0:T(4,128)} %gather_fusion, f32[16]{0:T(128)S(1)} %copy-done.5, f32[16]{0:T(128)S(1)} %broadcast_subtract_fusion), kind=kLoop, calls=%fused_computation.5 | loop fusion | flops 1179648 | bytes 4718720 | tf_op jit(solution)/shard_map/vmap()/add | solution.py:89
  107.5 1.6 %copy.20 = f32[3,16,16,512]{3,2,1,0:T(8,128)} copy(f32[3,16,16,512]{3,0,2,1:T(4,128)S(1)} %add_bitcast_fusion) | data formatting | bytes 3145728 | tf_op jit(solution)/shard_map/vmap()/add | solution.py:89
  (23 shorter events, 0.3 us)
Async XLA Ops:
  0.0 9.2 %copy-start.2 = (f32[3,16,16,512]{3,2,1,0:T(8,128)S(1)}, f32[3,16,16,512]{3,2,1,0:T(8,128)}, u32[]{:S(2)}) copy-start(f32[3,16,16,512]{3,2,1,0:T(8,128)} %param.10) | copy-start | bytes 4718596
  0.0 9.2 %copy-start.1 = (f32[3,16,16,512]{3,2,1,0:T(8,128)S(1)}, f32[3,16,16,512]{3,2,1,0:T(8,128)}, u32[]{:S(2)}) copy-start(f32[3,16,16,512]{3,2,1,0:T(8,128)} %param.11) | copy-start | bytes 4718596
  2.4 6.7 %collective-permute-start = (f32[6,1,16,512]{3,2,0,1:T(8,128)S(1)}, f32[6,1,16,512]{3,2,0,1:T(8,128)S(1)}, u32[]{:S(2)}, u32[]{:S(2)}) collective-permute-start(f32[6,1,16,512]{3,2,0,1:T(8,128)S(1)} %copy.23), channel_id=1, source_target_pairs={{0,4},{4,8},{8,12},{12,16},{16,20},{20,24},{24,28},{28,0},{1,5},{5... | collective-permute-start | bytes 589832 | tf_op jit(solution)/shard_map/ppermute | solution.py:19
  2.9 7.2 %collective-permute-start.1 = (f32[6,1,16,512]{3,2,0,1:T(8,128)S(1)}, f32[6,1,16,512]{3,2,0,1:T(8,128)S(1)}, u32[]{:S(2)}, u32[]{:S(2)}) collective-permute-start(f32[6,1,16,512]{3,2,0,1:T(8,128)S(1)} %copy.24), channel_id=1, source_target_pairs={{4,0},{8,4},{12,8},{16,12},{20,16},{24,20},{28,24},{0,28},{5,1},{9... | collective-permute-start | bytes 589832 | tf_op jit(solution)/shard_map/ppermute | solution.py:20
  9.2 6.1 %copy-start.3 = (s32[2]{0:T(128)S(1)}, s32[2]{0:T(128)}, u32[]{:S(2)}) copy-start(s32[2]{0:T(128)} %param.14) | copy-start | bytes 28
  11.3 10.1 %collective-permute-start.2 = (f32[6,18,1,512]{3,2,0,1:T(1,128)}, f32[6,18,1,512]{3,2,0,1:T(1,128)}, u32[]{:S(2)}, u32[]{:S(2)}) collective-permute-start(f32[6,18,1,512]{3,2,0,1:T(1,128)} %get-tuple-element.41), channel_id=1, source_target_pairs={{0,1},{1,2},{2,3},{3,0},{4,5},{5,6},{6,7},{7,4},{8,9},{9,10},{10,1... | collective-permute-start | bytes 663560 | tf_op jit(solution)/shard_map/ppermute | solution.py:19
  13.3 13.3 %collective-permute-start.3 = (f32[6,18,1,512]{3,2,0,1:T(1,128)}, f32[6,18,1,512]{3,2,0,1:T(1,128)}, u32[]{:S(2)}, u32[]{:S(2)}) collective-permute-start(f32[6,18,1,512]{3,2,0,1:T(1,128)} %get-tuple-element.42), channel_id=1, source_target_pairs={{1,0},{2,1},{3,2},{0,3},{5,4},{6,5},{7,6},{4,7},{9,8},{10,9},{11,1... | collective-permute-start | bytes 663560 | tf_op jit(solution)/shard_map/ppermute | solution.py:20
  18.5 13.2 %copy-start.4 = (f32[2]{0:T(128)S(1)}, f32[2]{0:T(128)}, u32[]{:S(2)}) copy-start(f32[2]{0:T(128)} %param.15) | copy-start | bytes 28
  28.6 2.4 %copy-start = (f32[6,18,18,512]{3,2,0,1:T(8,128)}, f32[6,18,18,512]{3,2,0,1:T(8,128)S(1)}, u32[]{:S(2)}) copy-start(f32[6,18,18,512]{3,2,0,1:T(8,128)S(1)} %pad_maximum_fusion) | copy-start | bytes 11943940
  31.0 7.6 %collective-permute-start.4 = (f32[6,8,512]{2,1,0:T(8,128)S(1)}, f32[6,8,512]{2,1,0:T(8,128)S(1)}, u32[]{:S(2)}, u32[]{:S(2)}) collective-permute-start(f32[6,8,512]{2,1,0:T(8,128)S(1)} %slice.423), channel_id=1, source_target_pairs={{0,1},{1,2},{2,3},{3,0},{4,5},{5,6},{6,7},{7,4},{8,9},{9,10},{10,1... | collective-permute-start | bytes 294920 | tf_op jit(solution)/shard_map/ppermute | solution.py:27
  41.1 14.1 %collective-permute-start.5 = (f32[6,8,512]{2,1,0:T(8,128)S(1)}, f32[6,8,512]{2,1,0:T(8,128)S(1)}, u32[]{:S(2)}, u32[]{:S(2)}) collective-permute-start(f32[6,8,512]{2,1,0:T(8,128)S(1)} %slice.427), channel_id=1, source_target_pairs={{0,3},{1,0},{2,1},{3,2},{4,7},{5,4},{6,5},{7,6},{8,11},{9,8},{10,9... | collective-permute-start | bytes 294920 | tf_op jit(solution)/shard_map/ppermute | solution.py:27
  65.8 3.9 %slice-start = ((s8[5308416]{0:T(1024)(128)(4,1)}), s8[4194304]{0:T(1024)(128)(4,1)S(1)}, s32[]{:S(2)}) async-start(s8[5308416]{0:T(1024)(128)(4,1)} %bitcast.64), calls=%async_computation | async-start | bytes 8388608
  68.6 1.4 %slice-start.1 = ((s8[5308416]{0:T(1024)(128)(4,1)}), s8[1114112]{0:T(1024)(128)(4,1)S(1)}, s32[]{:S(2)}) async-start(s8[5308416]{0:T(1024)(128)(4,1)} %bitcast.64), calls=%async_computation.1 | async-start | bytes 2228224
  75.5 2.1 %copy-start.5 = (f32[16]{0:T(128)S(1)}, f32[16]{0:T(128)}, u32[]{:S(2)}) copy-start(f32[16]{0:T(128)} %param.13) | copy-start | bytes 196
  75.5 2.1 %copy-start.6 = (s32[16]{0:T(128)S(1)}, s32[16]{0:T(128)}, u32[]{:S(2)}) copy-start(s32[16]{0:T(128)} %param.12) | copy-start | bytes 196
  77.3 19.0 %collective-permute-start.6 = (f32[3,16,7,512]{3,1,2,0:T(8,128)S(1)}, f32[3,16,7,512]{3,1,2,0:T(8,128)S(1)}, u32[]{:S(2)}, u32[]{:S(2)}) collective-permute-start(f32[3,16,7,512]{3,1,2,0:T(8,128)S(1)} %copy.18), channel_id=1, source_target_pairs={{0,1},{1,2},{2,3},{3,0},{4,5},{5,6},{6,7},{7,4},{8,9},{9,10},{10,1... | collective-permute-start | bytes 2064392 | tf_op jit(solution)/shard_map/ppermute | solution.py:27
where the time goes:
time: 110 us; the launch traced here: 109 us
  local copies, waits for them, and re-layouts  41.4 us (38%)
  waiting for transfers between devices  30.5 us (28%)
  other arithmetic  18.4 us (17%)
  starting transfers between devices  11.8 us (11%)
  between operations  7.04 us (6%)
    ppermute x3, waiting for transfers between devices, from_behind(): lax.ppermute(shard, axis, [(i, (i + by) % peers) for i in range(peers)])  18.6 us
    scatter x1, local copies, waits for them, and re-layouts, body(): padded.at[:, -1].set(jnp.where(last_block, remapped_high, high_rows))  8.59 us
    unnamed x22, local copies, waits for them, and re-layouts  8.29 us
    scatter x1, local copies, waits for them, and re-layouts, body(): padded = padded.at[:, 0].set(jnp.where(first_block, remapped_low, low_rows))  7.23 us
    ppermute x2, waiting for transfers between devices, with_halo(): before = lax.ppermute(last, axis, up)  6.23 us
    ppermute x2, waiting for transfers between devices, with_halo(): after = lax.ppermute(first, axis, down)  5.62 us
    ppermute x2, starting transfers between devices, with_halo(): after = lax.ppermute(first, axis, down)  4.98 us
    ppermute x3, starting transfers between devices, from_behind(): lax.ppermute(shard, axis, [(i, (i + by) % peers) for i in range(peers)])  4.39 us
  transfers between devices with their start and end apart: 7, of which 5 were waited for; matrix products, arithmetic and copies ran while one was open for 13% of the time, Pallas kernels for 0%

commit v1 on v0

v1 whole, which is shorter than its diff:
```python
import functools

import jax
import jax.numpy as jnp
from jax import lax
from jax.experimental import pallas as pl
from jax.experimental.pallas import tpu as pltpu
from jax.sharding import PartitionSpec as P

COURANT = 0.4
SCALE = COURANT * 0.125
MESH = pl.DeviceIdType.MESH


def kernel(
    blocks,
    phis,
    field,
    velocity,
    strip_shift,
    strip_frac,
    edge_shift,
    edge_frac,
    out,
    ext,
    low_raw,
    high_raw,
    low_corner,
    high_corner,
    row_send,
    row_recv,
    top_edges,
    bottom_edges,
    edge_send,
    edge_recv,
    updated,
    pack_a,
    pack_b,
    near_a,
    near_b,
    result,
    load_sem,
    store_sem,
    send_sem,
    recv_sem,
):
    b = lax.axis_index("blocks")
    p = lax.axis_index("phi")
    b_up = lax.rem(b + 1, blocks)
    b_down = lax.rem(b + blocks - 1, blocks)
    p_up = lax.rem(p + 1, phis)
    p_down = lax.rem(p + phis - 1, phis)
    first = b == 0
    last = b == blocks - 1
    strips = field.shape[1]
    wide = field.shape[3]

    loads = [
        pltpu.make_async_copy(
            source.at[:, :, rows, :],
            ext.at[part, 1 : strips + 1, pl.ds(8 + rows.start, 8), :],
            load_sem.at[n],
        )
        for n, (source, part, rows) in enumerate(
            (
                (field, slice(0, 3), slice(8, 16)),
                (velocity, slice(3, 6), slice(8, 16)),
                (field, slice(0, 3), slice(0, 8)),
                (velocity, slice(3, 6), slice(0, 8)),
            )
        )
    ]
    for load in loads:
        load.start()

    barrier = pltpu.get_barrier_semaphore()
    for device in ((b_up, p), (b_down, p), (b, p_up), (b, p_down)):
        pl.semaphore_signal(barrier, inc=1, device_id=device, device_id_type=MESH)

    @pl.when(first)
    def _():
        pl.semaphore_signal(barrier, inc=1, device_id=(b_down, p_down), device_id_type=MESH)

    @pl.when(last)
    def _():
        pl.semaphore_signal(barrier, inc=1, device_id=(b_up, p_up), device_id_type=MESH)

    pl.semaphore_wait(barrier, jnp.where(jnp.logical_or(first, last), 5, 4))

    def remote(n, source, target, device):
        return pltpu.make_async_remote_copy(
            src_ref=source,
            dst_ref=target,
            send_sem=send_sem.at[n],
            recv_sem=recv_sem.at[n],
            device_id=device,
            device_id_type=MESH,
        )

    end = strips - 1
    up_f = remote(0, field.at[1:3, end], low_raw.at[1:3, 8:24], (b_up, p))
    up_v = remote(1, velocity.at[:, end], low_raw.at[3:6, 8:24], (b_up, p))
    down_f = remote(2, field.at[:, 0], high_raw.at[0:3, 8:24], (b_down, p))
    down_v = remote(3, velocity.at[:, 0], high_raw.at[3:6, 8:24], (b_down, p))
    shear_up_f = remote(4, field.at[1:3, end, 8:16], low_raw.at[1:3, 0:8], (b_up, p_up))
    shear_up_v = remote(5, velocity.at[:, end, 8:16], low_raw.at[3:6, 0:8], (b_up, p_up))
    shear_down_f = remote(6, field.at[:, 0, 0:8], high_raw.at[0:3, 24:32], (b_down, p_down))
    shear_down_v = remote(7, velocity.at[:, 0, 0:8], high_raw.at[3:6, 24:32], (b_down, p_down))
    row_up = remote(8, row_send, row_recv, (b, p_up))
    corner_up = remote(9, row_recv.at[1:3, strips - 8 : strips], low_corner, (b_up, p))
    corner_down = remote(10, row_recv.at[0:3, 0:8], high_corner, (b_down, p))
    near_copy_a = remote(11, pack_a, near_a.at[:, 0:7, 0:8], (b, p_up))
    near_copy_b = remote(12, pack_b, near_b.at[:, 0:7, 0:8], (b, p_up))
    edges_down = remote(13, edge_send, edge_recv, (b, p_down))

    for copy in (up_f, up_v, down_f, down_v):
        copy.start()

    @pl.when(last)
    def _():
        shear_up_f.start()
        shear_up_v.start()

    @pl.when(first)
    def _():
        shear_down_f.start()
        shear_down_v.start()

    row_parts = (0, 3, 4, 5, 2)
    loads[0].wait()
    loads[1].wait()
    for n, part in enumerate(row_parts):
        for i in range(strips):
            row_send[n, i : i + 1, :] = ext[part, i + 1, 23:24, :]
    row_up.start()
    loads[2].wait()
    loads[3].wait()

    level = lax.broadcasted_iota(jnp.int32, (8, wide), 0)

    def below(values):
        return pltpu.roll(values, 1, axis=1)

    def above(values):
        return pltpu.roll(values, wide - 1, axis=1)

    def side_edges(i, row):
        here = lambda part: ext[part, i + 1, row : row + 8, :]
        inner = lambda part: ext[part, i, row : row + 8, :]
        here_low = lambda part: ext[part, i + 1, row - 1 : row + 7, :]
        inner_low = lambda part: ext[part, i, row - 1 : row + 7, :]
        fx = here(0)
        vx = here(3) + inner(3)
        vz = here(5) + inner(5)
        vx_all = vx + here_low(3) + inner_low(3)
        vy_all = here(4) + inner(4) + here_low(4) + inner_low(4)
        emf_z = vy_all * (fx + here_low(0)) - vx_all * (here(1) + inner(1))
        emf_y = (vx + below(vx)) * (here(2) + inner(2)) - (vz + below(vz)) * (fx + below(fx))
        return emf_z, emf_y

    def cross_edge(i, row):
        here = lambda part: ext[part, i + 1, row : row + 8, :]
        here_low = lambda part: ext[part, i + 1, row - 1 : row + 7, :]
        fy = here(1)
        vy = here(4) + here_low(4)
        vz = here(5) + here_low(5)
        return (vz + below(vz)) * (fy + below(fy)) - (vy + below(vy)) * (here(2) + here_low(2))

    def new_cells(i, row, emf_z, emf_y, emf_x, next_z, next_y, beyond_z, beyond_x):
        lift = lambda values, beyond: jnp.where(level == 7, beyond, pltpu.roll(values, 7, axis=0))
        new_x = ext[0, i + 1, row : row + 8, :] - SCALE * (
            (lift(emf_z, beyond_z) - emf_z) - (above(emf_y) - emf_y)
        )
        new_y = ext[1, i + 1, row : row + 8, :] - SCALE * (
            (above(emf_x) - emf_x) - (next_z - emf_z)
        )
        new_z = ext[2, i + 1, row : row + 8, :] - SCALE * (
            (next_y - emf_y) - (lift(emf_x, beyond_x) - emf_x)
        )
        return new_x, new_y, new_z

    def upper_rows(start, count, pack, offset):
        def step(n, carried):
            i = start + n
            emf_z, emf_y = carried
            next_z, next_y = side_edges(i + 1, 16)
            emf_x = cross_edge(i, 16)
            top_edges[0, i] = emf_z
            top_edges[1, i] = emf_x
            cells = new_cells(i, 16, emf_z, emf_y, emf_x, next_z, next_y, 0.0, 0.0)
            for part, values in enumerate(cells):
                updated[part, i, 8:16, :] = values
                pack[part, n + offset] = values
            return next_z, next_y

        lax.fori_loop(0, count, step, side_edges(start, 16))

    def spread_last(pack, strip):
        for part in range(3):
            for n in range(7):
                pack[part, n, 0:1, :] = updated[part, strip, 9 + n : 10 + n, :]

    quarter = strips // 4
    half = strips // 2
    upper_rows(quarter, half - 1, pack_a, 0)

    def one_upper(i):
        emf_z, emf_y = side_edges(i, 16)
        next_z, next_y = side_edges(i + 1, 16)
        emf_x = cross_edge(i, 16)
        top_edges[0, i] = emf_z
        top_edges[1, i] = emf_x
        cells = new_cells(i, 16, emf_z, emf_y, emf_x, next_z, next_y, 0.0, 0.0)
        for part, values in enumerate(cells):
            updated[part, i, 8:16, :] = values

    one_upper(quarter + half - 1)
    spread_last(pack_a, quarter + half - 1)
    near_copy_a.start()

    for copy in (up_f, up_v, down_f, down_v):
        copy.wait_recv()

    @pl.when(first)
    def _():
        shear_up_f.wait_recv()
        shear_up_v.wait_recv()
        shift = edge_shift[0]
        weight = edge_frac[0]
        for part in range(1, 6):
            rows = low_raw[part]
            mixed = (1.0 - weight) * rows + weight * pltpu.roll(rows, 1, axis=0)
            ext[part, 0, :, :] = pltpu.roll(mixed, shift, axis=0)

    @pl.when(jnp.logical_not(first))
    def _():
        for part in range(1, 6):
            ext[part, 0, 8:24, :] = low_raw[part, 8:24, :]

    @pl.when(last)
    def _():
        shear_down_f.wait_recv()
        shear_down_v.wait_recv()
        shift = edge_shift[1]
        weight = edge_frac[1]
        for part in range(6):
            rows = high_raw[part]
            mixed = (1.0 - weight) * rows + weight * pltpu.roll(rows, 31, axis=0)
            ext[part, strips + 1, 8:24, :] = pltpu.roll(mixed, lax.rem(32 - shift, 32), axis=0)[8:24]

    @pl.when(jnp.logical_not(last))
    def _():
        for part in range(6):
            ext[part, strips + 1, 8:24, :] = high_raw[part, 8:24, :]

    row_up.wait_recv()
    corner_up.start()
    corner_down.start()

    upper_rows(strips - quarter, quarter, pack_b, 0)
    upper_rows(0, quarter - 1, pack_b, quarter)
    one_upper(quarter - 1)
    spread_last(pack_b, quarter - 1)
    near_copy_b.start()

    for n, part in enumerate(row_parts):
        for i in range(strips):
            ext[part, i + 1, 7:8, :] = row_recv[n, i : i + 1, :]

    corner_up.wait_recv()
    corner_down.wait_recv()

    @pl.when(jnp.logical_not(first))
    def _():
        for n, part in enumerate((3, 4)):
            ext[part, 0, 7:8, :] = low_corner[n, 7:8, :]

    @pl.when(last)
    def _():
        shift = edge_shift[1]
        weight = edge_frac[1]
        for n, part in enumerate((0, 3, 4)):
            high_raw[part, 7:8, :] = high_corner[n, 0:1, :]
            rows = high_raw[part, 0:16, :]
            mixed = (1.0 - weight) * rows + weight * pltpu.roll(rows, 15, axis=0)
            ext[part, strips + 1, 7:8, :] = pltpu.roll(mixed, lax.rem(16 - shift, 16), axis=0)[7:8]

    @pl.when(jnp.logical_not(last))
    def _():
        for n, part in enumerate((0, 3, 4)):
            ext[part, strips + 1, 7:8, :] = high_corner[n, 0:1, :]

    def lower_rows(start, count, near, offset):
        def step(n, carried):
            i = start + n
            emf_z, emf_y = carried
            next_z, next_y = side_edges(i + 1, 8)
            emf_x = cross_edge(i, 8)
            bottom_edges[0, i] = emf_z
            bottom_edges[1, i] = emf_x
            cells = new_cells(
                i,
                8,
                emf_z,
                emf_y,
                emf_x,
                next_z,
                next_y,
                pltpu.roll(top_edges[0, i], 7, axis=0),
                pltpu.roll(top_edges[1, i], 7, axis=0),
            )
            for part, values in enumerate(cells):
                updated[part, i, 0:8, :] = values
                near[part, n + offset, 8:16, :] = values
            return next_z, next_y

        lax.fori_loop(0, count, step, side_edges(start, 8))

    lower_rows(0, quarter, near_b, quarter)
    lower_rows(quarter, half, near_a, 0)
    lower_rows(strips - quarter, quarter, near_b, 0)
    for n in range(2):
        for i in range(strips):
            edge_send[n, i : i + 1, :] = bottom_edges[n, i, 0:1, :]
    edges_down.start()

    edges_down.wait_recv()

    def blend_upper(i, _):
        updated[0, i, 15:16, :] = updated[0, i, 15:16, :] - SCALE * edge_recv[0, pl.ds(i, 1), :]
        updated[2, i, 15:16, :] = updated[2, i, 15:16, :] + SCALE * edge_recv[1, pl.ds(i, 1), :]
        shift = strip_shift[i]
        weight = strip_frac[i]
        for part in range(3):
            rows = updated[part, i]
            mixed = (1.0 - weight) * rows + weight * pltpu.roll(rows, 1, axis=0)
            result[part, i, 8:16, :] = pltpu.roll(mixed, shift, axis=0)[8:16]
        return 0

    lax.fori_loop(0, strips, blend_upper, 0)
    stores = [
        pltpu.make_async_copy(
            result.at[:, places, rows, :], out.at[:, places, rows, :], store_sem.at[n]
        )
        for n, (places, rows) in enumerate(
            (
                (slice(0, strips), slice(8, 16)),
                (slice(quarter, quarter + half), slice(0, 8)),
                (slice(strips - quarter, strips), slice(0, 8)),
                (slice(0, quarter), slice(0, 8)),
            )
        )
    ]
    stores[0].start()

    def blend_lower(near, start):
        for part in range(3):
            for n in range(7):
                near[part, 7, n + 1 : n + 2, :] = near[part, n, 0:1, :]

        def step(n, _):
            i = lax.rem(start + n, strips)
            near[0, n, 7:8, :] = near[0, n, 7:8, :] - SCALE * bottom_edges[0, i, 0:1, :]
            near[2, n, 7:8, :] = near[2, n, 7:8, :] + SCALE * bottom_edges[1, i, 0:1, :]
            shift = strip_shift[i]
            weight = strip_frac[i]
            for part in range(3):
                rows = near[part, n]
                mixed = (1.0 - weight) * rows + weight * pltpu.roll(rows, 1, axis=0)
                result[part, i, 0:8, :] = pltpu.roll(mixed, shift, axis=0)[8:16]
            return 0

        lax.fori_loop(0, half, step, 0)

    near_copy_a.wait_recv()
    blend_lower(near_a, quarter)
    stores[1].start()
    near_copy_b.wait_recv()
    blend_lower(near_b, strips - quarter)
    stores[2].start()
    stores[3].start()

    for copy in (up_f, up_v, down_f, down_v, row_up, corner_up, corner_down):
        copy.wait_send()
    for copy in (near_copy_a, near_copy_b, edges_down):
        copy.wait_send()

    @pl.when(last)
    def _():
        shear_up_f.wait_send()
        shear_up_v.wait_send()

    @pl.when(first)
    def _():
        shear_down_f.wait_send()
        shear_down_v.wait_send()

    for store in stores:
        store.wait()


def body(mesh_shape, field, velocity, strip_shift, strip_frac, edge_shift, edge_frac):
    parts, strips, azimuth, wide = field.shape
    half = strips // 2
    f32 = jnp.float32
    smem = pl.BlockSpec(memory_space=pltpu.SMEM)
    hbm = pl.BlockSpec(memory_space=pl.ANY)
    return pl.pallas_call(
        functools.partial(kernel, mesh_shape["blocks"], mesh_shape["phi"]),
        out_shape=jax.ShapeDtypeStruct(field.shape, f32),
        in_specs=[hbm, hbm, smem, smem, smem, smem],
        out_specs=hbm,
        scratch_shapes=[
            pltpu.VMEM((6, strips + 2, 8 + azimuth, wide), f32),
            pltpu.VMEM((6, 24, wide), f32),
            pltpu.VMEM((6, 32, wide), f32),
            pltpu.VMEM((2, 8, wide), f32),
            pltpu.VMEM((3, 8, wide), f32),
            pltpu.VMEM((5, strips, wide), f32),
            pltpu.VMEM((5, strips, wide), f32),
            pltpu.VMEM((2, strips, 8, wide), f32),
            pltpu.VMEM((2, strips, 8, wide), f32),
            pltpu.VMEM((2, strips, wide), f32),
            pltpu.VMEM((2, strips, wide), f32),
            pltpu.VMEM((3, strips, azimuth, wide), f32),
            pltpu.VMEM((3, 7, 8, wide), f32),
            pltpu.VMEM((3, 7, 8, wide), f32),
            pltpu.VMEM((3, half, 16, wide), f32),
            pltpu.VMEM((3, half, 16, wide), f32),
            pltpu.VMEM((3, strips, azimuth, wide), f32),
            pltpu.SemaphoreType.DMA((4,)),
            pltpu.SemaphoreType.DMA((4,)),
            pltpu.SemaphoreType.DMA((14,)),
            pltpu.SemaphoreType.DMA((14,)),
        ],
        compiler_params=pltpu.CompilerParams(
            collective_id=0, has_side_effects=True, vmem_limit_bytes=40 * 1024 * 1024
        ),
    )(field, velocity, strip_shift, strip_frac, edge_shift, edge_frac)


def solution(mesh):
    placed = (
        P(None, "blocks", "phi", None),
        P(None, "blocks", "phi", None),
        P("blocks"),
        P("blocks"),
        P(),
        P(),
    )
    return jax.shard_map(
        functools.partial(body, dict(mesh.shape)),
        mesh=mesh,
        in_specs=placed,
        out_specs=P(None, "blocks", "phi", None),
        check_vma=False,
    )
```

time: 110 us -> 37.6 us (0.34)
  local copies, waits for them, and re-layouts: 41.4 us -> 6.58 us
  Pallas kernels: 0 us -> 30.8 us
  waiting for transfers between devices: 30.5 us -> 0 us
  other arithmetic: 18.4 us -> 0 us
  starting transfers between devices: 11.8 us -> 0 us
  between operations: 7.04 us -> 0.02 us
    pallas_call x0 -> x1, Pallas kernels: none -> 30.8 us  [body(): pl.pallas_call(functools.partial(kernel, mesh_shape['blocks'], mesh_shape...]
    ppermute x7 -> x0, waiting for transfers between devices: 30.5 us -> none  [the longest x3 18.6 us: from_behind(): lax.ppermute(shard, axis, [(i, (i + by) % peers) for i in range(peers)])]
    scatter x2 -> x0, local copies, waits for them, and re-layouts: 15.8 us -> none  [the longest x1 8.59 us: body(): padded.at[:, -1].set(jnp.where(last_block, remapped_high, high_rows))]
    ppermute x7 -> x0, starting transfers between devices: 11.8 us -> none  [the longest x2 4.98 us: with_halo(): after = lax.ppermute(first, axis, down)]
    slice x21 -> x0, local copies, waits for them, and re-layouts: 6.47 us -> none  [the longest x1 2.56 us: ct_update(): radial_vy = flow_y[1:-1]]
    gather x2 -> x0, local copies, waits for them, and re-layouts: 6 us -> none  [the longest x1 3.02 us: blend_rows(): trailing = lax.dynamic_slice_in_dim(extended, far_start, length, axis=1)]
    concatenate x2 -> x0, other arithmetic: 4.41 us -> none  [the longest x1 2.35 us: body(): stacked = jnp.concatenate([field, velocity], axis=0)]
    add x3 -> x0, other arithmetic: 3.36 us -> none  [the longest x1 2.95 us: blend_rows(): return (1.0 - weight) * leading + weight * trailing]
  transfers between devices with their start and end apart: 7 -> 0, of which waited for: 5 -> 0; matrix products, arithmetic and copies ran while one was open for 13% -> 0% of each run, Pallas kernels for 0% -> 0%
where the time goes in v1:
time: 37.6 us; the launch traced here: 37.4 us
  Pallas kernels  30.8 us (82%)
  local copies, waits for them, and re-layouts  6.58 us (18%)
    pallas_call x1, Pallas kernels, body(): pl.pallas_call(functools.partial(kernel, mesh_shape['blocks'], mesh_shape...  30.8 us
    unnamed x13, local copies, waits for them, and re-layouts  6.58 us

profile of v1, /device:TPU:0, one launch (start us, length us, event | category | flops | bytes accessed | tf_op | source)
XLA Modules:
  0.0 37.4 jit_solution(1961738346751237590)
XLA Ops:
  0.0 0.0 copy-start
  0.0 1.4 %copy-done = f32[3,16,16,512]{3,2,1,0:T(8,128)S(1)} copy-done((f32[3,16,16,512]{3,2,1,0:T(8,128)S(1)}, f32[3,16,16,512]{3,2,1,0:T(8,128)}, u32[]{:S(2)}) %copy-start) | copy-done | bytes 1572888
  1.4 0.0 copy-start.1
  1.4 1.4 %copy-done.1 = f32[3,16,16,512]{3,2,1,0:T(8,128)S(1)} copy-done((f32[3,16,16,512]{3,2,1,0:T(8,128)S(1)}, f32[3,16,16,512]{3,2,1,0:T(8,128)}, u32[]{:S(2)}) %copy-start.1) | copy-done | bytes 1572888
  2.8 0.0 copy-start.2
  2.8 0.7 %copy-done.2 = s32[16]{0:T(128)S(1)} copy-done((s32[16]{0:T(128)S(1)}, s32[16]{0:T(128)}, u32[]{:S(2)}) %copy-start.2) | copy-done | bytes 88
  3.5 0.0 copy-start.3
  3.5 0.7 %copy-done.3 = f32[16]{0:T(128)S(1)} copy-done((f32[16]{0:T(128)S(1)}, f32[16]{0:T(128)}, u32[]{:S(2)}) %copy-start.3) | copy-done | bytes 88
  4.1 0.0 copy-start.4
  4.1 0.7 %copy-done.4 = s32[2]{0:T(128)S(1)} copy-done((s32[2]{0:T(128)S(1)}, s32[2]{0:T(128)}, u32[]{:S(2)}) %copy-start.4) | copy-done | bytes 32
  4.8 0.0 copy-start.5
  4.8 0.7 %copy-done.5 = f32[2]{0:T(128)S(1)} copy-done((f32[2]{0:T(128)S(1)}, f32[2]{0:T(128)}, u32[]{:S(2)}) %copy-start.5) | copy-done | bytes 32
  5.4 30.8 %shard_map.64 = f32[3,16,16,512]{3,2,1,0:T(8,128)S(1)} custom-call(f32[3,16,16,512]{3,2,1,0:T(8,128)S(1)} %copy-done, f32[3,16,16,512]{3,2,1,0:T(8,128)S(1)} %copy-done.1, s32[16]{0:T(128)S(1)} %copy-done.2, f32[16]{0:T(128)S(1)} %copy-done.3, s32[2]{0:T(128)S(1)} %copy-done.4, f32[2]{0:T(128)S(1)} %copy-done.5), custom_call_target="tpu_custom_call" | custom-call | tf_op jit(solution)/shard_map/pallas_call | solution.py:408
  36.2 1.1 %copy.8 = f32[3,16,16,512]{3,2,1,0:T(8,128)} copy(f32[3,16,16,512]{3,2,1,0:T(8,128)S(1)} %shard_map.64) | data formatting | bytes 3145728
Async XLA Ops:
  0.0 1.4 %copy-start = (f32[3,16,16,512]{3,2,1,0:T(8,128)S(1)}, f32[3,16,16,512]{3,2,1,0:T(8,128)}, u32[]{:S(2)}) copy-start(f32[3,16,16,512]{3,2,1,0:T(8,128)} %field.1) | copy-start | bytes 4718596
  1.4 1.4 %copy-start.1 = (f32[3,16,16,512]{3,2,1,0:T(8,128)S(1)}, f32[3,16,16,512]{3,2,1,0:T(8,128)}, u32[]{:S(2)}) copy-start(f32[3,16,16,512]{3,2,1,0:T(8,128)} %velocity.1) | copy-start | bytes 4718596
  2.8 0.7 %copy-start.2 = (s32[16]{0:T(128)S(1)}, s32[16]{0:T(128)}, u32[]{:S(2)}) copy-start(s32[16]{0:T(128)} %strip_shift.1) | copy-start | bytes 196
  3.5 0.7 %copy-start.3 = (f32[16]{0:T(128)S(1)}, f32[16]{0:T(128)}, u32[]{:S(2)}) copy-start(f32[16]{0:T(128)} %strip_frac.1) | copy-start | bytes 196
  4.1 0.7 %copy-start.4 = (s32[2]{0:T(128)S(1)}, s32[2]{0:T(128)}, u32[]{:S(2)}) copy-start(s32[2]{0:T(128)} %edge_shift.1) | copy-start | bytes 28
  4.8 0.7 %copy-start.5 = (f32[2]{0:T(128)S(1)}, f32[2]{0:T(128)}, u32[]{:S(2)}) copy-start(f32[2]{0:T(128)} %edge_frac.1) | copy-start | bytes 28

commit v2 on v1

--- a/solution.py
+++ b/solution.py
@@ -17,10 +17,10 @@
     phis,
     field,
     velocity,
-    strip_shift,
-    strip_frac,
-    edge_shift,
-    edge_frac,
+    shift_in,
+    frac_in,
+    edge_shift_in,
+    edge_frac_in,
     out,
     ext,
     low_raw,
@@ -39,6 +39,10 @@
     near_a,
     near_b,
     result,
+    strip_shift,
+    strip_frac,
+    edge_shift,
+    edge_frac,
     load_sem,
     store_sem,
     send_sem,
@@ -72,6 +76,19 @@
     ]
     for load in loads:
         load.start()
+    scalars = [
+        pltpu.make_async_copy(source, target, load_sem.at[4 + n])
+        for n, (source, target) in enumerate(
+            (
+                (shift_in, strip_shift),
+                (frac_in, strip_frac),
+                (edge_shift_in, edge_shift),
+                (edge_frac_in, edge_frac),
+            )
+        )
+    ]
+    for copy in scalars:
+        copy.start()
 
     barrier = pltpu.get_barrier_semaphore()
     for device in ((b_up, p), (b_down, p), (b, p_up), (b, p_down)):
@@ -218,6 +235,8 @@
     spread_last(pack_a, quarter + half - 1)
     near_copy_a.start()
 
+    for copy in scalars:
+        copy.wait()
     for copy in (up_f, up_v, down_f, down_v):
         copy.wait_recv()
 
@@ -403,12 +422,11 @@
     parts, strips, azimuth, wide = field.shape
     half = strips // 2
     f32 = jnp.float32
-    smem = pl.BlockSpec(memory_space=pltpu.SMEM)
-    hbm = pl.BlockSpec(memory_space=pl.ANY)
+    hbm = pl.BlockSpec(memory_space=pltpu.HBM)
     return pl.pallas_call(
         functools.partial(kernel, mesh_shape["blocks"], mesh_shape["phi"]),
         out_shape=jax.ShapeDtypeStruct(field.shape, f32),
-        in_specs=[hbm, hbm, smem, smem, smem, smem],
+        in_specs=[hbm] * 6,
         out_specs=hbm,
         scratch_shapes=[
             pltpu.VMEM((6, strips + 2, 8 + azimuth, wide), f32),
@@ -428,13 +446,17 @@
             pltpu.VMEM((3, half, 16, wide), f32),
             pltpu.VMEM((3, half, 16, wide), f32),
             pltpu.VMEM((3, strips, azimuth, wide), f32),
-            pltpu.SemaphoreType.DMA((4,)),
+            pltpu.SMEM(strip_shift.shape, jnp.int32),
+            pltpu.SMEM(strip_frac.shape, f32),
+            pltpu.SMEM(edge_shift.shape, jnp.int32),
+            pltpu.SMEM(edge_frac.shape, f32),
+            pltpu.SemaphoreType.DMA((8,)),
             pltpu.SemaphoreType.DMA((4,)),
             pltpu.SemaphoreType.DMA((14,)),
             pltpu.SemaphoreType.DMA((14,)),
         ],
         compiler_params=pltpu.CompilerParams(
-            collective_id=0, has_side_effects=True, vmem_limit_bytes=40 * 1024 * 1024
+            collective_id=0, has_side_effects=True, vmem_limit_bytes=64 * 1024 * 1024 - 65536
         ),
     )(field, velocity, strip_shift, strip_frac, edge_shift, edge_frac)
 

time: 37.6 us -> 33.4 us (0.89)
  local copies, waits for them, and re-layouts: 6.58 us -> 2.77 us
    unnamed x13 -> x1, local copies, waits for them, and re-layouts: 6.58 us -> 2.77 us
where the time goes in v2:
time: 33.4 us; the launch traced here: 33.3 us
  Pallas kernels  30.5 us (91%)
  local copies, waits for them, and re-layouts  2.77 us (8%)
    pallas_call x1, Pallas kernels, body(): pl.pallas_call(functools.partial(kernel, mesh_shape['blocks'], mesh_shape...  30.5 us
    unnamed x1, local copies, waits for them, and re-layouts  2.77 us

profile of v2, /device:TPU:0, one launch (start us, length us, event | category | flops | bytes accessed | tf_op | source)
XLA Modules:
  0.0 33.3 jit_solution(7972566042198570958)
XLA Ops:
  0.0 30.5 %shard_map.64 = f32[3,16,16,512]{3,2,1,0:T(8,128)} custom-call(f32[3,16,16,512]{3,2,1,0:T(8,128)} %field.1, f32[3,16,16,512]{3,2,1,0:T(8,128)} %velocity.1, s32[16]{0:T(128)} %shift_in.1, f32[16]{0:T(128)} %frac_in.1, s32[2]{0:T(128)} %edge_shift_in.1, f32[2]{0:T(128)} %edge_frac_in.1), custom_call_target="tpu_custom_call" | custom-call | tf_op jit(solution)/shard_map/pallas_call | solution.py:426
  30.5 2.8 %copy.8 = f32[3,16,16,512]{3,2,1,0:T(8,128)} copy(f32[3,16,16,512]{3,2,1,0:T(8,128)} %shard_map.64) | data formatting | bytes 3145728

commit v3 on v2

--- a/solution.py
+++ b/solution.py
@@ -38,13 +38,11 @@
     pack_b,
     near_a,
     near_b,
-    result,
     strip_shift,
     strip_frac,
     edge_shift,
     edge_frac,
     load_sem,
-    store_sem,
     send_sem,
     recv_sem,
 ):
@@ -74,7 +72,7 @@
             )
         )
     ]
-    for load in loads:
+    for load in loads[0:2]:
         load.start()
     scalars = [
         pltpu.make_async_copy(source, target, load_sem.at[4 + n])
@@ -121,14 +119,18 @@
     down_v = remote(3, velocity.at[:, 0], high_raw.at[3:6, 8:24], (b_down, p))
     shear_up_f = remote(4, field.at[1:3, end, 8:16], low_raw.at[1:3, 0:8], (b_up, p_up))
     shear_up_v = remote(5, velocity.at[:, end, 8:16], low_raw.at[3:6, 0:8], (b_up, p_up))
-    shear_down_f = remote(6, field.at[:, 0, 0:8], high_raw.at[0:3, 24:32], (b_down, p_down))
-    shear_down_v = remote(7, velocity.at[:, 0, 0:8], high_raw.at[3:6, 24:32], (b_down, p_down))
+    shear_down = remote(6, high_raw.at[:, 8:16], high_raw.at[:, 24:32], (b, p_down))
     row_up = remote(8, row_send, row_recv, (b, p_up))
     corner_up = remote(9, row_recv.at[1:3, strips - 8 : strips], low_corner, (b_up, p))
     corner_down = remote(10, row_recv.at[0:3, 0:8], high_corner, (b_down, p))
-    near_copy_a = remote(11, pack_a, near_a.at[:, 0:7, 0:8], (b, p_up))
-    near_copy_b = remote(12, pack_b, near_b.at[:, 0:7, 0:8], (b, p_up))
-    edges_down = remote(13, edge_send, edge_recv, (b, p_down))
+    edges_down = remote(7, edge_send, edge_recv, (b, p_down))
+    near_copy_a, near_copy_b = (
+        [
+            remote(n + part, pack.at[part], near.at[part, 0:7, 0:8], (b, p_up))
+            for part in range(3)
+        ]
+        for n, pack, near in ((11, pack_a, near_a), (14, pack_b, near_b))
+    )
 
     for copy in (up_f, up_v, down_f, down_v):
         copy.start()
@@ -137,15 +139,12 @@
     def _():
         shear_up_f.start()
         shear_up_v.start()
-
-    @pl.when(first)
-    def _():
-        shear_down_f.start()
-        shear_down_v.start()
 
     row_parts = (0, 3, 4, 5, 2)
     loads[0].wait()
     loads[1].wait()
+    loads[2].start()
+    loads[3].start()
     for n, part in enumerate(row_parts):
         for i in range(strips):
             row_send[n, i : i + 1, :] = ext[part, i + 1, 23:24, :]
@@ -233,7 +232,8 @@
 
     one_upper(quarter + half - 1)
     spread_last(pack_a, quarter + half - 1)
-    near_copy_a.start()
+    for copy in near_copy_a:
+        copy.start()
 
     for copy in scalars:
         copy.wait()
@@ -258,8 +258,8 @@
 
     @pl.when(last)
     def _():
-        shear_down_f.wait_recv()
-        shear_down_v.wait_recv()
+        shear_down.start()
+        shear_down.wait_recv()
         shift = edge_shift[1]
         weight = edge_frac[1]
         for part in range(6):
@@ -280,7 +280,8 @@
     upper_rows(0, quarter - 1, pack_b, quarter)
     one_upper(quarter - 1)
     spread_last(pack_b, quarter - 1)
-    near_copy_b.start()
+    for copy in near_copy_b:
+        copy.start()
 
     for n, part in enumerate(row_parts):
         for i in range(strips):
@@ -353,69 +354,46 @@
         for part in range(3):
             rows = updated[part, i]
             mixed = (1.0 - weight) * rows + weight * pltpu.roll(rows, 1, axis=0)
-            result[part, i, 8:16, :] = pltpu.roll(mixed, shift, axis=0)[8:16]
+            out[part, i, 8:16, :] = pltpu.roll(mixed, shift, axis=0)[8:16]
         return 0
 
     lax.fori_loop(0, strips, blend_upper, 0)
-    stores = [
-        pltpu.make_async_copy(
-            result.at[:, places, rows, :], out.at[:, places, rows, :], store_sem.at[n]
-        )
-        for n, (places, rows) in enumerate(
-            (
-                (slice(0, strips), slice(8, 16)),
-                (slice(quarter, quarter + half), slice(0, 8)),
-                (slice(strips - quarter, strips), slice(0, 8)),
-                (slice(0, quarter), slice(0, 8)),
-            )
-        )
-    ]
-    stores[0].start()
-
-    def blend_lower(near, start):
-        for part in range(3):
-            for n in range(7):
-                near[part, 7, n + 1 : n + 2, :] = near[part, n, 0:1, :]
+    def blend_lower(near, start, part):
+        for n in range(7):
+            near[part, 7, n + 1 : n + 2, :] = near[part, n, 0:1, :]
 
         def step(n, _):
             i = lax.rem(start + n, strips)
-            near[0, n, 7:8, :] = near[0, n, 7:8, :] - SCALE * bottom_edges[0, i, 0:1, :]
-            near[2, n, 7:8, :] = near[2, n, 7:8, :] + SCALE * bottom_edges[1, i, 0:1, :]
-            shift = strip_shift[i]
+            rows = near[part, n]
+            if part == 0:
+                rows = rows - jnp.where(lowest, SCALE * bottom_edges[0, i, 0:1, :], 0.0)
+            if part == 2:
+                rows = rows + jnp.where(lowest, SCALE * bottom_edges[1, i, 0:1, :], 0.0)
             weight = strip_frac[i]
-            for part in range(3):
-                rows = near[part, n]
-                mixed = (1.0 - weight) * rows + weight * pltpu.roll(rows, 1, axis=0)
-                result[part, i, 0:8, :] = pltpu.roll(mixed, shift, axis=0)[8:16]
+            mixed = (1.0 - weight) * rows + weight * pltpu.roll(rows, 1, axis=0)
+            out[part, i, 0:8, :] = pltpu.roll(mixed, strip_shift[i], axis=0)[8:16]
             return 0
 
         lax.fori_loop(0, half, step, 0)
 
-    near_copy_a.wait_recv()
-    blend_lower(near_a, quarter)
-    stores[1].start()
-    near_copy_b.wait_recv()
-    blend_lower(near_b, strips - quarter)
-    stores[2].start()
-    stores[3].start()
+    lowest = lax.broadcasted_iota(jnp.int32, (16, wide), 0) == 7
+    for part in range(3):
+        near_copy_a[part].wait_recv()
+        blend_lower(near_a, quarter, part)
+    for part in range(3):
+        near_copy_b[part].wait_recv()
+        blend_lower(near_b, strips - quarter, part)
 
     for copy in (up_f, up_v, down_f, down_v, row_up, corner_up, corner_down):
         copy.wait_send()
-    for copy in (near_copy_a, near_copy_b, edges_down):
+    for copy in (*near_copy_a, *near_copy_b, edges_down):
         copy.wait_send()
 
     @pl.when(last)
     def _():
         shear_up_f.wait_send()
         shear_up_v.wait_send()
-
-    @pl.when(first)
-    def _():
-        shear_down_f.wait_send()
-        shear_down_v.wait_send()
-
-    for store in stores:
-        store.wait()
+        shear_down.wait_send()
 
 
 def body(mesh_shape, field, velocity, strip_shift, strip_frac, edge_shift, edge_frac):
@@ -425,9 +403,9 @@
     hbm = pl.BlockSpec(memory_space=pltpu.HBM)
     return pl.pallas_call(
         functools.partial(kernel, mesh_shape["blocks"], mesh_shape["phi"]),
-        out_shape=jax.ShapeDtypeStruct(field.shape, f32),
+        out_shape=pltpu.VMEM(field.shape, f32),
         in_specs=[hbm] * 6,
-        out_specs=hbm,
+        out_specs=pl.BlockSpec(memory_space=pltpu.VMEM),
         scratch_shapes=[
             pltpu.VMEM((6, strips + 2, 8 + azimuth, wide), f32),
             pltpu.VMEM((6, 24, wide), f32),
@@ -445,18 +423,16 @@
             pltpu.VMEM((3, 7, 8, wide), f32),
             pltpu.VMEM((3, half, 16, wide), f32),
             pltpu.VMEM((3, half, 16, wide), f32),
-            pltpu.VMEM((3, strips, azimuth, wide), f32),
             pltpu.SMEM(strip_shift.shape, jnp.int32),
             pltpu.SMEM(strip_frac.shape, f32),
             pltpu.SMEM(edge_shift.shape, jnp.int32),
             pltpu.SMEM(edge_frac.shape, f32),
             pltpu.SemaphoreType.DMA((8,)),
-            pltpu.SemaphoreType.DMA((4,)),
-            pltpu.SemaphoreType.DMA((14,)),
-            pltpu.SemaphoreType.DMA((14,)),
+            pltpu.SemaphoreType.DMA((17,)),
+            pltpu.SemaphoreType.DMA((17,)),
         ],
         compiler_params=pltpu.CompilerParams(
-            collective_id=0, has_side_effects=True, vmem_limit_bytes=64 * 1024 * 1024 - 65536
+            collective_id=0, has_side_effects=True, vmem_limit_bytes=62 * 1024 * 1024
         ),
     )(field, velocity, strip_shift, strip_frac, edge_shift, edge_frac)
 

time: 33.4 us -> 32.7 us (0.979)
  local copies, waits for them, and re-layouts: 2.77 us -> 1.15 us
  Pallas kernels: 30.5 us -> 31.4 us
    unnamed x1, local copies, waits for them, and re-layouts: 2.77 us -> 1.15 us
    pallas_call x1, Pallas kernels: 30.5 us -> 31.4 us  [body(): pl.pallas_call(functools.partial(kernel, mesh_shape['blocks'], mesh_shape...]
where the time goes in v3:
time: 32.7 us; the launch traced here: 32.5 us
  Pallas kernels  31.4 us (96%)
  local copies, waits for them, and re-layouts  1.15 us (4%)
    pallas_call x1, Pallas kernels, body(): pl.pallas_call(functools.partial(kernel, mesh_shape['blocks'], mesh_shape...  31.4 us
    unnamed x1, local copies, waits for them, and re-layouts  1.15 us

profile of v3, /device:TPU:0, one launch (start us, length us, event | category | flops | bytes accessed | tf_op | source)
XLA Modules:
  0.0 32.5 jit_solution(17103002398237607406)
XLA Ops:
  0.0 31.4 %shard_map.64 = f32[3,16,16,512]{3,2,1,0:T(8,128)S(1)} custom-call(f32[3,16,16,512]{3,2,1,0:T(8,128)} %field.1, f32[3,16,16,512]{3,2,1,0:T(8,128)} %velocity.1, s32[16]{0:T(128)} %shift_in.1, f32[16]{0:T(128)} %frac_in.1, s32[2]{0:T(128)} %edge_shift_in.1, f32[2]{0:T(128)} %edge_frac_in.1), custom_call_target="tpu_custom_call" | custom-call | tf_op jit(solution)/shard_map/pallas_call | solution.py:404
  31.4 1.1 %copy.8 = f32[3,16,16,512]{3,2,1,0:T(8,128)} copy(f32[3,16,16,512]{3,2,1,0:T(8,128)S(1)} %shard_map.64) | data formatting | bytes 3145728

commit v4 on v3

--- a/solution.py
+++ b/solution.py
@@ -119,26 +119,33 @@
     down_v = remote(3, velocity.at[:, 0], high_raw.at[3:6, 8:24], (b_down, p))
     shear_up_f = remote(4, field.at[1:3, end, 8:16], low_raw.at[1:3, 0:8], (b_up, p_up))
     shear_up_v = remote(5, velocity.at[:, end, 8:16], low_raw.at[3:6, 0:8], (b_up, p_up))
-    shear_down = remote(6, high_raw.at[:, 8:16], high_raw.at[:, 24:32], (b, p_down))
+    shear_down_f = remote(6, field.at[:, 0, 0:8], high_raw.at[0:3, 24:32], (b_down, p_down))
+    shear_down_v = remote(17, velocity.at[:, 0, 0:8], high_raw.at[3:6, 24:32], (b_down, p_down))
     row_up = remote(8, row_send, row_recv, (b, p_up))
     corner_up = remote(9, row_recv.at[1:3, strips - 8 : strips], low_corner, (b_up, p))
     corner_down = remote(10, row_recv.at[0:3, 0:8], high_corner, (b_down, p))
     edges_down = remote(7, edge_send, edge_recv, (b, p_down))
-    near_copy_a, near_copy_b = (
-        [
-            remote(n + part, pack.at[part], near.at[part, 0:7, 0:8], (b, p_up))
-            for part in range(3)
-        ]
-        for n, pack, near in ((11, pack_a, near_a), (14, pack_b, near_b))
-    )
+    near_copy_a = [
+        remote(11 + part, pack_a.at[part], near_a.at[part, 0:7, 0:8], (b, p_up))
+        for part in range(3)
+    ]
+    near_copy_b = [
+        remote(14 + n, pack_b.at[:, tiles], near_b.at[:, tiles, 0:8], (b, p_up))
+        for n, tiles in enumerate((slice(0, 3), slice(5, 7), slice(3, 5)))
+    ]
+
+    @pl.when(last)
+    def _():
+        shear_up_f.start()
+        shear_up_v.start()
+
+    @pl.when(first)
+    def _():
+        shear_down_f.start()
+        shear_down_v.start()
 
     for copy in (up_f, up_v, down_f, down_v):
         copy.start()
-
-    @pl.when(last)
-    def _():
-        shear_up_f.start()
-        shear_up_v.start()
 
     row_parts = (0, 3, 4, 5, 2)
     loads[0].wait()
@@ -211,9 +218,9 @@
 
         lax.fori_loop(0, count, step, side_edges(start, 16))
 
-    def spread_last(pack, strip):
+    def spread_last(pack, strip, tiles):
         for part in range(3):
-            for n in range(7):
+            for n in tiles:
                 pack[part, n, 0:1, :] = updated[part, strip, 9 + n : 10 + n, :]
 
     quarter = strips // 4
@@ -231,9 +238,16 @@
             updated[part, i, 8:16, :] = values
 
     one_upper(quarter + half - 1)
-    spread_last(pack_a, quarter + half - 1)
+    spread_last(pack_a, quarter + half - 1, range(7))
     for copy in near_copy_a:
         copy.start()
+
+    upper_rows(strips - quarter, quarter - 1, pack_b, 0)
+    upper_rows(1, quarter - 2, pack_b, quarter + 1)
+    one_upper(quarter - 1)
+    spread_last(pack_b, quarter - 1, (0, 1, 2, 5, 6))
+    near_copy_b[0].start()
+    near_copy_b[1].start()
 
     for copy in scalars:
         copy.wait()
@@ -258,8 +272,8 @@
 
     @pl.when(last)
     def _():
-        shear_down.start()
-        shear_down.wait_recv()
+        shear_down_f.wait_recv()
+        shear_down_v.wait_recv()
         shift = edge_shift[1]
         weight = edge_frac[1]
         for part in range(6):
@@ -276,12 +290,10 @@
     corner_up.start()
     corner_down.start()
 
-    upper_rows(strips - quarter, quarter, pack_b, 0)
-    upper_rows(0, quarter - 1, pack_b, quarter)
-    one_upper(quarter - 1)
-    spread_last(pack_b, quarter - 1)
-    for copy in near_copy_b:
-        copy.start()
+    upper_rows(strips - 1, 1, pack_b, quarter - 1)
+    upper_rows(0, 1, pack_b, quarter)
+    spread_last(pack_b, quarter - 1, (3, 4))
+    near_copy_b[2].start()
 
     for n, part in enumerate(row_parts):
         for i in range(strips):
@@ -380,8 +392,9 @@
     for part in range(3):
         near_copy_a[part].wait_recv()
         blend_lower(near_a, quarter, part)
+    for copy in near_copy_b:
+        copy.wait_recv()
     for part in range(3):
-        near_copy_b[part].wait_recv()
         blend_lower(near_b, strips - quarter, part)
 
     for copy in (up_f, up_v, down_f, down_v, row_up, corner_up, corner_down):
@@ -393,7 +406,11 @@
     def _():
         shear_up_f.wait_send()
         shear_up_v.wait_send()
-        shear_down.wait_send()
+
+    @pl.when(first)
+    def _():
+        shear_down_f.wait_send()
+        shear_down_v.wait_send()
 
 
 def body(mesh_shape, field, velocity, strip_shift, strip_frac, edge_shift, edge_frac):
@@ -428,8 +445,8 @@
             pltpu.SMEM(edge_shift.shape, jnp.int32),
             pltpu.SMEM(edge_frac.shape, f32),
             pltpu.SemaphoreType.DMA((8,)),
-            pltpu.SemaphoreType.DMA((17,)),
-            pltpu.SemaphoreType.DMA((17,)),
+            pltpu.SemaphoreType.DMA((18,)),
+            pltpu.SemaphoreType.DMA((18,)),
         ],
         compiler_params=pltpu.CompilerParams(
             collective_id=0, has_side_effects=True, vmem_limit_bytes=62 * 1024 * 1024

time: 32.7 us -> 31.4 us (0.960)
  Pallas kernels: 31.4 us -> 30.1 us
    pallas_call x1, Pallas kernels: 31.4 us -> 30.1 us  [body(): pl.pallas_call(functools.partial(kernel, mesh_shape['blocks'], mesh_shape...]
where the time goes in v4:
time: 31.4 us; the launch traced here: 31.3 us
  Pallas kernels  30.1 us (96%)
  local copies, waits for them, and re-layouts  1.15 us (4%)
    pallas_call x1, Pallas kernels, body(): pl.pallas_call(functools.partial(kernel, mesh_shape['blocks'], mesh_shape...  30.1 us
    unnamed x1, local copies, waits for them, and re-layouts  1.15 us

profile of v4, /device:TPU:0, one launch (start us, length us, event | category | flops | bytes accessed | tf_op | source)
XLA Modules:
  0.0 31.3 jit_solution(4626405257563664651)
XLA Ops:
  0.0 30.1 %shard_map.64 = f32[3,16,16,512]{3,2,1,0:T(8,128)S(1)} custom-call(f32[3,16,16,512]{3,2,1,0:T(8,128)} %field.1, f32[3,16,16,512]{3,2,1,0:T(8,128)} %velocity.1, s32[16]{0:T(128)} %shift_in.1, f32[16]{0:T(128)} %frac_in.1, s32[2]{0:T(128)} %edge_shift_in.1, f32[2]{0:T(128)} %edge_frac_in.1), custom_call_target="tpu_custom_call" | custom-call | tf_op jit(solution)/shard_map/pallas_call | solution.py:421
  30.1 1.1 %copy.8 = f32[3,16,16,512]{3,2,1,0:T(8,128)} copy(f32[3,16,16,512]{3,2,1,0:T(8,128)S(1)} %shard_map.64) | data formatting | bytes 3145728
